TPU v7x, 256 devices: a whole 4x4x8 slice. The times are simulated.
256 devices in a mesh: rows: 4 (over y), vocab: 64 (over z, x, core).
Axes of the slice: x: 4, y: 4, z: 8, core: 2. Of those that a mesh axis runs over, the one named last changes fastest.
Arguments:
- hidden: bfloat16 [2048, 7168], P('vocab', 'rows'), may hold values from -50 to 50
- head_weight: bfloat16 [7168, 65536], P('rows', 'vocab'), may hold values from -2 to 2
- draft_probs: float32 [2048, 65536], P(('rows', 'vocab')), may hold values from 0 to 1, as said below
- draft_ids: int32 [2048, 1], P('rows'), may hold values from 0 to 65535
Outputs:
- residual: float32 [2048, 65536], P('rows', 'vocab')
- accept_ratio: float32 [2048], P('rows')
Inputs may be any that keep to these rules, and one draw needn't show every extreme that they name: Each row of draft_probs sums to one, up to rounding.
All inputs are finite; a program needn't handle non-finite values.
Results may differ from a plain program's by a relative error of at most 0.0012.
Values may be sent and summed in bfloat16 or wider, within the bound.
A program may use at most 128 MiB of HBM per device.

v0:
```python
import jax
import jax.numpy as jnp
from jax import lax
from jax.sharding import PartitionSpec as P

mass_floor = 0.05


def local(hidden, head_weight, draft_probs, draft_ids):
    vocab_width = head_weight.shape[1]
    gathered = lax.all_gather(hidden, "vocab", axis=0, tiled=True)
    logits = lax.psum_scatter(
        jnp.dot(gathered, head_weight, preferred_element_type=jnp.float32),
        "rows",
        scatter_dimension=0,
        tiled=True,
    )
    draft = lax.all_to_all(draft_probs, "vocab", split_axis=1, concat_axis=0, tiled=True)
    offset = lax.axis_index("vocab") * vocab_width
    columns = offset + lax.iota(jnp.int32, vocab_width)
    chosen = columns[None, :] == draft_ids
    picked_draft_local = jnp.sum(jnp.where(chosen, draft, 0.0), axis=1)
    top = lax.pmax(jnp.max(logits, axis=1), "vocab")
    weights = jnp.exp(logits - top[:, None])
    total, picked_weight, picked_draft = lax.psum(
        (
            jnp.sum(weights, axis=1),
            jnp.sum(jnp.where(chosen, weights, 0.0), axis=1),
            picked_draft_local,
        ),
        "vocab",
    )
    target = weights / total[:, None]
    accept_ratio = jnp.minimum(jnp.float32(1.0), picked_weight / total / picked_draft)
    excess = jnp.maximum(target - draft, jnp.float32(0.0))
    mass = lax.psum(jnp.sum(excess, axis=1), "vocab")
    residual = excess / jnp.maximum(mass, mass_floor)[:, None]
    return (residual, accept_ratio)


def solution(mesh):
    in_specs = (P("vocab", "rows"), P("rows", "vocab"), P(("rows", "vocab"), None), P("rows", None))
    out_specs = (P("rows", "vocab"), P("rows"))
    return jax.shard_map(local, mesh=mesh, in_specs=in_specs, out_specs=out_specs, check_vma=False)
```

profile of v0, /device:TPU:1, one launch (start us, length us, event | category | flops | bytes accessed | tf_op | source)
XLA Modules:
  0.0 585.6 jit_solution(14806477488791530628)
XLA Ops:
  7.2 0.0 all-gather.2.cloned.1.call-start
  7.2 0.7 all-gather.2.cloned.1.call-update
  7.9 0.0 reduce-scatter.2.cloned.1.call-start
  7.9 89.0 %all-gather.2.cloned.1.call-done = bf16[2048,1792]{1,0:T(8,128)(2,1)} async-done(((bf16[32,1792]{1,0:T(8,128)(2,1)}), bf16[2048,1792]{1,0:T(8,128)(2,1)}) %all-gather.2.cloned.1.call-update) | async-done | bytes 7340048 | tf_op jit(solution)/shard_map/all_gather | solution.py:11
  97.0 13.0 %fusion.6 = f32[2048,1024]{1,0:T(8,128)} fusion(bf16[2048,1792]{1,0:T(8,128)(2,1)} %all-gather.2.cloned.1.call-done, bf16[1792,1024]{1,0:T(8,128)(2,1)} %param.5), kind=kOutput, calls=%fused_computation.13 | convolution fusion | flops 7516192768 | bytes 19398656 | tf_op jit(solution)/shard_map/dot_general | solution.py:13
  110.0 0.0 reduce-scatter.2.cloned.1.call-update
  110.1 0.0 copy-start.2
  110.1 5.8 all-to-all-start
  115.8 0.5 broadcast.17
  116.3 0.0 copy-done.2
  116.3 0.7 reduce.4
  117.0 0.1 eq.29
  117.1 48.4 %all-to-all-done = f32[8,64,1024]{2,0,1:T(8,128)S(1)} async-done(((f32[8,64,1024]{2,0,1:T(8,128)}), f32[8,64,1024]{2,0,1:T(8,128)S(1)}, u32[]{:S(2)}, u32[]{:S(2)}) %all-to-all-start) | async-done | bytes 2097184 | tf_op jit(solution)/shard_map/all_to_all | solution.py:18
  165.5 0.0 copy-start.1
  165.5 0.3 fusion.1
  165.8 0.1 reduce_sum.42
  165.9 0.9 copy-done.1
  166.8 22.8 %reduce-scatter.2.cloned.1.call-done = f32[512,1024]{1,0:T(8,128)} async-done(((f32[2048,1024]{1,0:T(8,128)}), f32[512,1024]{1,0:T(8,128)}) %reduce-scatter.2.cloned.1.call-update) | async-done | bytes 2097168 | tf_op jit(solution)/shard_map/reduce_scatter | solution.py:12
  189.7 0.0 copy-start
  189.7 1.9 reduce_max.9
  191.6 124.6 %pmax.7 = f32[512]{0:T(512)S(1)} all-reduce(f32[512]{0:T(512)S(1)} %reduce_max.9), channel_id=1, replica_groups=mesh['rows'=4,'vocab'=64] {'vocab'}, use_global_device_ids=true, to_apply=%region_2.3 | all-reduce | flops 512 | bytes 4096 | tf_op jit(solution)/shard_map/pmax | solution.py:23
  316.1 0.0 copy-done
  316.1 0.7 select_reduce_fusion
  316.8 128.5 %psum.28 = f32[512]{0:T(512)S(1)} all-reduce(f32[512]{0:T(512)S(1)} %get-tuple-element.3), channel_id=1, replica_groups=mesh['rows'=4,'vocab'=64] {'vocab'}, use_global_device_ids=true, to_apply=%region_4.5 | all-reduce | flops 512 | bytes 4096 | tf_op jit(solution)/shard_map/psum | solution.py:25
  445.3 3.6 fusion.4
  449.0 126.0 %all-reduce = (f32[512]{0:T(512)S(1)}, f32[512]{0:T(512)S(1)}, f32[512]{0:T(512)S(1)}) all-reduce(f32[512]{0:T(512)S(1)} %get-tuple-element.7, f32[512]{0:T(512)S(1)} %get-tuple-element.2, f32[512]{0:T(512)S(1)} %reduce_sum.42), channel_id=1, replica_groups=mesh['rows'=4,'vocab'=64] {'vocab'}, use_global_device_ids=true, to_apply=%region_6.7 | all-reduce | flops 1536 | bytes 12288 | tf_op jit(solution)/shard_map/psum | solution.py:36
  575.0 0.6 fusion.3
  575.6 3.2 broadcast_divide_fusion
  (1 shorter events, 0.0 us)
Async XLA Ops:
  7.2 89.8 %all-gather.2.cloned.1.call-start = ((), (), s32[]{:S(2)}) async-start(), calls=%async_computation.2 | async-start | bytes 7454720 | tf_op jit(solution)/shard_map/all_gather | solution.py:11
  7.9 181.8 %reduce-scatter.2.cloned.1.call-start = ((), (), s32[]{:S(2)}) async-start(), calls=%async_computation.3 | async-start | bytes 10485760 | tf_op jit(solution)/shard_map/reduce_scatter | solution.py:12
  110.1 6.3 %copy-start.2 = (s32[512,1]{0,1:T(1,128)S(1)}, s32[512,1]{0,1:T(1,128)}, u32[]{:S(2)}) copy-start(s32[512,1]{0,1:T(1,128)} %param.7) | copy-start | bytes 6148
  110.1 55.4 %all-to-all-start = ((f32[8,64,1024]{2,0,1:T(8,128)}), f32[8,64,1024]{2,0,1:T(8,128)S(1)}, u32[]{:S(2)}, u32[]{:S(2)}) async-start(f32[8,64,1024]{2,0,1:T(8,128)} %bitcast.15), calls=%async_computation.1 | async-start | bytes 4194304 | tf_op jit(solution)/shard_map/all_to_all | solution.py:18
  165.5 1.3 copy-start.1
  189.7 126.5 %copy-start = (f32[512,1024]{1,0:T(8,128)S(1)}, f32[512,1024]{1,0:T(8,128)}, u32[]{:S(2)}) copy-start(f32[512,1024]{1,0:T(8,128)} %reduce-scatter.2.cloned.1.call-done) | copy-start | bytes 6291460
Sparse Core Ops, SparseCore 0:
  10.7 86.1 all-gather.1
  110.2 79.4 reduce-scatter.1
where the time goes:
time: 586 us
  blocking collectives  379 us (65%)
  waiting for transfers between devices  161 us (27%)
  between operations  14.1 us (2%)
  matrix products  13 us (2%)
  other arithmetic  11 us (2%)
    psum x1, blocking collectives, local(): lax.psum((jnp.sum(weights, axis=1), jnp.sum(jnp.where(chosen, weights, 0....  129 us
    psum x1, blocking collectives, local(): mass = lax.psum(jnp.sum(excess, axis=1), 'vocab')  126 us
    pmax x1, blocking collectives, local(): top = lax.pmax(jnp.max(logits, axis=1), 'vocab')  125 us
    all_gather x1, waiting for transfers between devices, local(): gathered = lax.all_gather(hidden, 'vocab', axis=0, tiled=True)  89 us
    all_to_all x1, waiting for transfers between devices, local(): lax.all_to_all(draft_probs, 'vocab', split_axis=1, concat_axis=0, tiled=T...  48.4 us
    reduce_scatter x1, waiting for transfers between devices, local(): lax.psum_scatter(jnp.dot(gathered, head_weight, preferred_element_type=jn...  22.8 us
    dot_general x1, matrix products, local(): jnp.dot(gathered, head_weight, preferred_element_type=jnp.float32)  13 us
  transfers between devices with their start and end apart: 3, of which 3 were waited for; matrix products, arithmetic and copies ran while one was open for 0% of the time, Pallas kernels for 0%

commit v1 on v0

v1 whole, which is shorter than its diff:
```python
import jax
import jax.numpy as jnp
from jax import lax
from jax.experimental import pallas as pl
from jax.experimental.pallas import tpu as pltpu
from jax.sharding import PartitionSpec as P

MESH = pl.DeviceIdType.MESH
F32 = jnp.float32
mass_floor = 0.05

NY, NZ, NX, NC = 4, 8, 4, 2
NV = NZ * NX * NC
SHARD = 32
FEATURES = 1792
SPLIT = 1024
WIDTH = 1024
HALF = 512
ROWS = 256

ZF = pl.ds(0, SPLIT)
ZF_LO, ZF_HI = pl.ds(0, SPLIT // 2), pl.ds(SPLIT // 2, SPLIT // 2)
XF = pl.ds(SPLIT, FEATURES - SPLIT)
XF_LO = pl.ds(SPLIT, (FEATURES - SPLIT) // 2)
XF_HI = pl.ds((FEATURES + SPLIT) // 2, (FEATURES - SPLIT) // 2)

LEVELS = 8388600.0
STEPS = 64.0
PACKED = 384

ZZ, ZX, XX, XZ, SIB, AG_SEMS = 0, 8, 40, 44, 60, 68


def to_lanes(block):
    return jnp.transpose(block, (1, 0))


def to_rows(row):
    return jnp.transpose(jnp.broadcast_to(row, (128, row.shape[1])), (1, 0))


def tile8(block):
    return jnp.concatenate([block] * 8, axis=1)


def fold8(block):
    total = block[:, 0:128]
    for i in range(1, 8):
        total = total + block[:, 128 * i : 128 * (i + 1)]
    return total


def unpack(words, scale):
    a, b, c = (words[:, 128 * i : 128 * (i + 1)] for i in range(3))
    d = (a & 255) | ((b & 255) << 8) | ((c << 24) >> 8)
    return jnp.concatenate([q.astype(F32) * scale for q in (a >> 8, b >> 8, c >> 8, d)], axis=1)


def kernel(
    hid, w_hbm, draft_hbm, ids_ref, out_hbm, acc_ref,
    G, W, part, leg, fin, pk, dr, E, idc, colm, cola, colb, colc, colk, S,
    ag_send, ag_recv, y_send, y_recv, st_send, st_recv, dr_send, dr_recv, loc,
):
    r = lax.axis_index("rows")
    v = lax.axis_index("vocab")
    z = v // (NX * NC)
    x = (v // NC) % NX
    c = v % NC

    def vid(zz, xx, cc):
        return zz * (NX * NC) + xx * NC + cc

    def around(d):
        return (z + NZ + d) % NZ

    zp, zm = around(1), around(-1)
    xp, xm, xo = (x + 1) % NX, (x + NX - 1) % NX, (x + 2) % NX
    rp, rm = (r + 1) % NY, (r + NY - 1) % NY
    to_zp, to_zm = (r, vid(zp, x, c)), (r, vid(zm, x, c))
    to_xp, to_xm = (r, vid(z, xp, c)), (r, vid(z, xm, c))
    to_sib = (r, vid(z, x, 1 - c))
    order = [around(d) for d in (0, -1, 1, -2, 2, -3, 3, 4)]

    own_copy = pltpu.make_async_copy(hid, G.at[z, x, c], loc.at[0])
    own_copy.start()
    w_copy = pltpu.make_async_copy(w_hbm, W, loc.at[1])
    w_copy.start()

    barrier = pltpu.get_barrier_semaphore()
    for ry in (rp, rm):
        pl.semaphore_signal(barrier, inc=1, device_id=(ry, v), device_id_type=MESH)

    @pl.loop(1, NV)
    def _(k):
        pl.semaphore_signal(barrier, inc=1, device_id=(r, (v + k) % NV), device_id_type=MESH)

    pl.semaphore_wait(barrier, NV + 1)

    sent = []

    def remote(src, dst, ss, rs, dev):
        return pltpu.make_async_remote_copy(
            src_ref=src, dst_ref=dst, send_sem=ss, recv_sem=rs, device_id=dev, device_id_type=MESH
        )

    def wait_recv(region, rs):
        remote(region, region, rs, rs, to_sib).wait_recv()

    def spread(region, sem, dev, src=None):
        cp = remote(region if src is None else src, region, ag_send.at[sem], ag_recv.at[sem], dev)
        cp.start()
        sent.append(cp)

    def arrived(region, sem):
        wait_recv(region, ag_recv.at[sem])

    def zf(zz, xx, cols=ZF):
        return G.at[zz, xx, c, :, cols]

    def zf_x_send(j):
        src = hid.at[:, ZF] if j == 0 else None
        spread(zf(order[j], x), ZX + 4 * j, to_xp, src)
        spread(zf(order[j], x), ZX + 4 * j + 1, to_xm, src)

    def zf_x_mid(j):
        zz = order[j]
        arrived(zf(zz, xm), ZX + 4 * j)
        spread(zf(zz, xm, ZF_LO), ZX + 4 * j + 2, to_xp)
        arrived(zf(zz, xp), ZX + 4 * j + 1)
        spread(zf(zz, xp, ZF_HI), ZX + 4 * j + 3, to_xm)

    def zf_x_end(j):
        zz = order[j]
        arrived(zf(zz, xo, ZF_LO), ZX + 4 * j + 2)
        arrived(zf(zz, xo, ZF_HI), ZX + 4 * j + 3)

    def zf_z(d):
        if d == 0:
            spread(zf(z, x), ZZ, to_zp, hid.at[:, ZF])
            spread(zf(z, x), ZZ + 1, to_zm, hid.at[:, ZF])
            zf_x_send(0)
            return
        if d == 4:
            arrived(zf(order[7], x, ZF_LO), ZZ + 6)
            arrived(zf(order[7], x, ZF_HI), ZZ + 7)
            zf_x_send(7)
            return
        za, zb = order[2 * d - 1], order[2 * d]
        arrived(zf(za, x), ZZ + 2 * d - 2)
        spread(zf(za, x, ZF_LO if d == 3 else ZF), ZZ + 2 * d, to_zp)
        zf_x_send(2 * d - 1)
        arrived(zf(zb, x), ZZ + 2 * d - 1)
        spread(zf(zb, x, ZF_HI if d == 3 else ZF), ZZ + 2 * d + 1, to_zm)
        zf_x_send(2 * d)

    def xf(xx, cols=XF):
        return G.at[z, xx, c, :, cols]

    def xfs(zz, cols=XF):
        return G.at[zz, :, c, :, cols]

    def xf_x_start():
        spread(xf(x), XX, to_xp, hid.at[:, XF])
        spread(xf(x), XX + 1, to_xm, hid.at[:, XF])
        spread(xf(x), XX + 2, (r, vid(z, xo, c)), hid.at[:, XF])

    def xf_x_end():
        arrived(xf(xm), XX)
        arrived(xf(xp), XX + 1)
        arrived(xf(xo), XX + 2)

    def xf_z(d):
        if d == 0:
            spread(xfs(z, XF_LO), XZ, to_zp)
            spread(xfs(z, XF_HI), XZ + 3, to_zm)
            spread(xfs(z, XF_HI), XZ + 1, to_zp)
            spread(xfs(z, XF_LO), XZ + 2, to_zm)
            return
        if d == 4:
            arrived(xfs(order[7], XF_LO), XZ + 12)
            arrived(xfs(order[7], XF_HI), XZ + 13)
            return
        za, zb = order[2 * d - 1], order[2 * d]
        o = XZ + 4 * d
        arrived(xfs(za, XF_LO), o - 4)
        spread(xfs(za, XF_LO), o, to_zp)
        arrived(xfs(zb, XF_HI), o - 1)
        spread(xfs(zb, XF_HI), o + (1 if d == 3 else 3), to_zm)
        arrived(xfs(za, XF_HI), o - 3)
        arrived(xfs(zb, XF_LO), o - 2)
        if d < 3:
            spread(xfs(za, XF_HI), o + 1, to_zp)
            spread(xfs(zb, XF_LO), o + 2, to_zm)

    def sib(j):
        spread(G.at[order[j], :, c], SIB + j, to_sib)

    def sib_wait(j):
        arrived(G.at[order[j], :, 1 - c], SIB + j)

    def role(zz):
        return (zz // 2 - r + NY) % NY, zz % 2

    def far_left(q, j):
        return remote(pk.at[0, q, 0], leg.at[0, q], y_send.at[2 * j], y_recv.at[q], (rp, v))

    def far_right(q, j):
        return remote(pk.at[0, q, 1], leg.at[1, q], y_send.at[2 * j + 1], y_recv.at[2 + q], (rm, v))

    def near_right(q, j):
        return remote(pk.at[1, q, 1], fin.at[q, 0, 1], y_send.at[2 * j + 1], y_recv.at[4 + q], (rp, v))

    def near_left(q, j):
        return remote(pk.at[1, q, 0], fin.at[q, 1, 0], y_send.at[2 * j], y_recv.at[6 + q], (rm, v))

    def pack(zz, side, dst):
        @pl.loop(0, 4)
        def _(i):
            rows = pl.ds(pl.multiple_of(i * 64, 64), 64)
            block = part[zz, side, rows]
            unit = jnp.floor(jnp.max(jnp.abs(block), axis=1, keepdims=True) * STEPS) + 1.0
            colk[0, rows] = jnp.broadcast_to(unit, (64, 128))
            level = jnp.round(block * (LEVELS * STEPS / unit)).astype(jnp.int32)
            a, b, c, d = (level[:, 128 * k : 128 * (k + 1)] for k in range(4))
            dst[rows, 0:128] = (a << 8) | (d & 255)
            dst[rows, 128:256] = (b << 8) | ((d >> 8) & 255)
            dst[rows, 256:384] = (c << 8) | ((d >> 16) & 255)

        dst[ROWS : ROWS + 1, 0:ROWS] = to_lanes(colk[0])[0:1].astype(jnp.int32)

    def scales(src, k):
        colk[k] = to_rows(src[ROWS : ROWS + 1, 0:ROWS].astype(F32)) * (1.0 / (LEVELS * STEPS))

    def product(j):
        zz = order[j]

        @pl.loop(0, 4)
        def _(n):
            lhs = G[zz].reshape(ROWS, FEATURES)
            rhs = W[:, pl.ds(pl.multiple_of(n * 256, 256), 256)]
            res = jnp.dot(lhs, rhs, preferred_element_type=F32)
            part[zz, n // 2, :, pl.ds(pl.multiple_of((n % 2) * 256, 256), 256)] = res

        d, q = role(zz)

        @pl.when(d == 2)
        def _():
            pack(zz, 0, pk.at[0, q, 0])
            far_left(q, j).start()
            pack(zz, 1, pk.at[0, q, 1])
            far_right(q, j).start()

        @pl.when(d == 1)
        def _():
            pack(zz, 1, pk.at[1, q, 1])
            near_right(q, j).start()

        @pl.when(d == 3)
        def _():
            pack(zz, 0, pk.at[1, q, 0])
            near_left(q, j).start()

    def product_sent(j):
        d, q = role(order[j])

        @pl.when(d >= 2)
        def _():
            far_left(q, j).wait_send()

        @pl.when((d == 1) | (d == 2))
        def _():
            far_right(q, j).wait_send()

    def add_leg(zz, side, q):
        scales(leg.at[side, q], 1)

        @pl.loop(0, 4)
        def _(i):
            rows = pl.ds(pl.multiple_of(i * 64, 64), 64)
            part[zz, side, rows] = part[zz, side, rows] + unpack(leg[side, q, rows], colk[1, rows])

    def onward(q):
        for side, owner in ((0, rp), (1, rm)):
            zz = 2 * owner + q
            wait_recv(leg.at[side, q], y_recv.at[2 * side + q])
            add_leg(zz, side, q)
            pack(zz, side, pk.at[2, q, side])
            cp = remote(
                pk.at[2, q, side], fin.at[q, side, side], y_send.at[16 + 2 * side + q],
                y_recv.at[8 + 2 * side + q], (owner, v),
            )
            cp.start()
            sent.append(cp)

    def fin_wait(q):
        wait_recv(fin.at[q, 0, 1], y_recv.at[4 + q])
        wait_recv(fin.at[q, 1, 0], y_recv.at[6 + q])
        wait_recv(fin.at[q, 0, 0], y_recv.at[8 + q])
        wait_recv(fin.at[q, 1, 1], y_recv.at[10 + q])

    def exchange(q, e):
        mine = S.at[q, e, v]

        @pl.loop(0, NZ)
        def _(i):
            dz = 4 + (1 - 2 * (i % 2)) * ((i + 1) // 2)
            zz = (z + dz) % NZ
            for dx in (2, 1, 3, 0):
                for dc in (1, 0):
                    cp = remote(
                        mine, mine, st_send.at[q, e], st_recv.at[q, e],
                        (r, vid(zz, (x + dx) % NX, (c + dc) % NC)),
                    )
                    if dx == 0 and dc == 0:
                        pl.when(i < NZ - 1)(cp.start)
                    else:
                        cp.start()

    def exchange_wait(q, e):
        wait_recv(S.at[q, e, pl.ds(0, NV - 1)], st_recv.at[q, e])

    def exchange_sent(q, e):
        region = S.at[q, e, pl.ds(0, NV - 1)]
        remote(region, region, st_send.at[q, e], st_recv.at[q, e], to_sib).wait_send()

    def local_stats(q):
        zz = 2 * r + q
        for side in range(2):
            for k in range(2):
                scales(fin.at[q, k, side], 2 * side + k)

        @pl.loop(0, 8)
        def _(i):
            rows = pl.ds(pl.multiple_of(i * 32, 32), 32)
            halves = []
            for side in range(2):
                below = unpack(fin[q, 0, side, rows], colk[2 * side, rows])
                above = unpack(fin[q, 1, side, rows], colk[2 * side + 1, rows])
                halves.append(part[zz, side, rows] + (below + above))
            logit = jnp.concatenate(halves, axis=1)
            top = jnp.max(logit, axis=1, keepdims=True)
            weight = jnp.exp(logit - top)
            E[q, rows] = weight
            colm[q, rows] = jnp.broadcast_to(top, (32, 128))
            cola[rows] = fold8(weight)

        S[q, 0, v, :, 0:ROWS] = to_lanes(colm[q])[0:1]
        S[q, 0, v, :, ROWS : 2 * ROWS] = jnp.sum(to_lanes(cola[...]), axis=0, keepdims=True)

    columns = (lax.broadcasted_iota(jnp.int32, (32, WIDTH), 1) + v * WIDTH).astype(F32)

    def local_excess(q):
        exchange_wait(q, 0)
        tops = S[q, 0, :, :, 0:ROWS]
        sums = S[q, 0, :, :, ROWS : 2 * ROWS]
        top = jnp.max(tops, axis=0)
        total = jnp.sum(sums * jnp.exp(tops - top[None]), axis=0)
        own_top = to_lanes(colm[q])[0:1]
        colm[q] = to_rows(jnp.exp(own_top - top) / total)

        @pl.loop(0, 8)
        def _(i):
            rows = pl.ds(pl.multiple_of(i * 32, 32), 32)
            all_rows = pl.ds(pl.multiple_of(q * ROWS + i * 32, 32), 32)
            target = E[q, rows] * tile8(colm[q, rows])
            draft = dr[all_rows]
            chosen = columns == tile8(idc[all_rows])
            excess = jnp.maximum(target - draft, 0.0)
            E[q, rows] = excess
            cola[rows] = fold8(excess)
            colb[rows] = fold8(jnp.where(chosen, target, 0.0))
            colc[rows] = fold8(jnp.where(chosen, draft, 0.0))

        mass, picked, drafted = (
            jnp.sum(to_lanes(ref[...]), axis=0, keepdims=True) for ref in (cola, colb, colc)
        )
        token = jnp.concatenate([ids_ref[2 * q : 2 * q + 1], ids_ref[2 * q + 1 : 2 * q + 2]], axis=1)
        here = (token >= v * WIDTH) & (token < (v + 1) * WIDTH)
        ratio = jnp.where(here, jnp.minimum(1.0, picked / drafted), 0.0)
        S[q, 1, v, :, 0:ROWS] = mass
        S[q, 1, v, :, ROWS : 2 * ROWS] = ratio

    def finish(q):
        exchange_wait(q, 1)
        both = jnp.sum(S[q, 1], axis=0)
        acc_ref[q : q + 1] = both[:, ROWS : 2 * ROWS]
        colm[q] = to_rows(1.0 / jnp.maximum(both[:, 0:ROWS], mass_floor))

        @pl.loop(0, 8)
        def _(i):
            rows = pl.ds(pl.multiple_of(i * 32, 32), 32)
            E[q, rows] = E[q, rows] * tile8(colm[q, rows])

        cp = pltpu.make_async_copy(E.at[q], out_hbm.at[pl.ds(q * ROWS, ROWS)], loc.at[2 + q])
        cp.start()
        return cp

    spot = dr.at[pl.ds(pl.multiple_of(v * 8, 8), 8)]

    def draft_send():
        pltpu.make_async_copy(
            draft_hbm.at[:, pl.ds(pl.multiple_of(v * WIDTH, WIDTH), WIDTH)], spot, dr_recv
        ).start()

        @pl.loop(1, NV)
        def _(k):
            d = (v + k) % NV
            remote(
                draft_hbm.at[:, pl.ds(pl.multiple_of(d * WIDTH, WIDTH), WIDTH)], spot, dr_send, dr_recv, (r, d)
            ).start()

    zf_z(0)
    xf_x_start()
    zf_x_mid(0)
    own_copy.wait()
    xf_x_end()
    xf_z(0)
    zf_z(1)
    zf_x_end(0)
    sib(0)
    zf_x_mid(1)
    zf_x_mid(2)
    zf_z(2)
    w_copy.wait()
    sib_wait(0)
    product(0)
    for d in (1, 2, 3):
        a, b = 2 * d - 1, 2 * d
        xf_z(d)
        zf_x_end(a)
        zf_x_end(b)
        sib(a)
        sib(b)
        if d == 1:
            for j in range(4):
                idc[128 * j : 128 * j + 128] = to_rows(ids_ref[j : j + 1].astype(F32))
        if d < 3:
            zf_x_mid(a + 2)
            zf_x_mid(b + 2)
            zf_z(d + 2)
        else:
            zf_x_mid(7)
            draft_send()
        sib_wait(a)
        product(a)
        sib_wait(b)
        product(b)
    xf_z(4)
    zf_x_end(7)
    sib(7)
    sib_wait(7)
    product(7)
    onward(0)
    onward(1)
    fin_wait(0)
    local_stats(0)
    exchange(0, 0)
    pltpu.make_async_copy(dr, dr, dr_recv).wait()
    local_excess(0)
    exchange(0, 1)
    out0 = finish(0)
    fin_wait(1)
    local_stats(1)
    exchange(1, 0)
    local_excess(1)
    exchange(1, 1)
    out1 = finish(1)

    for cp in sent:
        cp.wait_send()
    for j in range(8):
        product_sent(j)
    for q in range(2):
        for e in range(2):
            exchange_sent(q, e)
    some = draft_hbm.at[:, pl.ds(0, (NV - 1) * WIDTH)]
    remote(some, some, dr_send, dr_recv, to_sib).wait_send()
    out0.wait()
    out1.wait()


def local(hidden, head_weight, draft_probs, draft_ids):
    dma = pltpu.SemaphoreType.DMA
    residual, accept = pl.pallas_call(
        kernel,
        out_shape=(
            jax.ShapeDtypeStruct((2 * ROWS, WIDTH), F32),
            jax.ShapeDtypeStruct((2, ROWS), F32),
        ),
        in_specs=[pl.BlockSpec(memory_space=pltpu.HBM)] * 3 + [pl.BlockSpec(memory_space=pltpu.VMEM)],
        out_specs=(pl.BlockSpec(memory_space=pltpu.HBM), pl.BlockSpec(memory_space=pltpu.VMEM)),
        scratch_shapes=[
            pltpu.VMEM((NZ, NX, NC, SHARD, FEATURES), jnp.bfloat16),
            pltpu.VMEM((FEATURES, WIDTH), jnp.bfloat16),
            pltpu.VMEM((NZ, 2, ROWS, HALF), F32),
            pltpu.VMEM((2, 2, ROWS + 8, PACKED), jnp.int32),
            pltpu.VMEM((2, 2, 2, ROWS + 8, PACKED), jnp.int32),
            pltpu.VMEM((3, 2, 2, ROWS + 8, PACKED), jnp.int32),
            pltpu.VMEM((2 * ROWS, WIDTH), F32),
            pltpu.VMEM((2, ROWS, WIDTH), F32),
            pltpu.VMEM((2 * ROWS, 128), F32),
            pltpu.VMEM((2, ROWS, 128), F32),
            pltpu.VMEM((ROWS, 128), F32),
            pltpu.VMEM((ROWS, 128), F32),
            pltpu.VMEM((ROWS, 128), F32),
            pltpu.VMEM((4, ROWS, 128), F32),
            pltpu.VMEM((2, 2, NV, 1, 2 * ROWS), F32),
            dma((AG_SEMS,)),
            dma((AG_SEMS,)),
            dma((20,)),
            dma((12,)),
            dma((2, 2)),
            dma((2, 2)),
            dma,
            dma,
            dma((4,)),
        ],
        compiler_params=pltpu.CompilerParams(
            collective_id=0, has_side_effects=True, vmem_limit_bytes=48 * 1024 * 1024
        ),
        cost_estimate=pl.CostEstimate(flops=7_516_192_768, bytes_accessed=16_000_000, transcendentals=524_288),
    )(hidden, head_weight, draft_probs, draft_ids.reshape(4, 128))
    return residual, accept.reshape(2 * ROWS)


def solution(mesh):
    in_specs = (P("vocab", "rows"), P("rows", "vocab"), P(("rows", "vocab"), None), P("rows", None))
    out_specs = (P("rows", "vocab"), P("rows"))
    return jax.shard_map(local, mesh=mesh, in_specs=in_specs, out_specs=out_specs, check_vma=False)
```

time: 586 us -> 129 us (0.22)
  blocking collectives: 379 us -> 0 us
  waiting for transfers between devices: 161 us -> 0 us
  Pallas kernels: 0 us -> 123 us
  between operations: 14.1 us -> 0.65 us
  matrix products: 13 us -> 0 us
  other arithmetic: 11 us -> 0 us
    psum x2 -> x0, blocking collectives: 255 us -> none  [the longest x1 129 us: local(): lax.psum((jnp.sum(weights, axis=1), jnp.sum(jnp.where(chosen, weights, 0....]
    pmax x1 -> x0, blocking collectives: 125 us -> none  [local(): top = lax.pmax(jnp.max(logits, axis=1), 'vocab')]
    pallas_call x0 -> x1, Pallas kernels: none -> 123 us  [local(): pl.pallas_call(kernel, out_shape=(jax.ShapeDtypeStruct((2 * ROWS, WIDTH),...]
    all_gather x1 -> x0, waiting for transfers between devices: 89 us -> none  [local(): gathered = lax.all_gather(hidden, 'vocab', axis=0, tiled=True)]
    all_to_all x1 -> x0, waiting for transfers between devices: 48.4 us -> none  [local(): lax.all_to_all(draft_probs, 'vocab', split_axis=1, concat_axis=0, tiled=T...]
    reduce_scatter x1 -> x0, waiting for transfers between devices: 22.8 us -> none  [local(): lax.psum_scatter(jnp.dot(gathered, head_weight, preferred_element_type=jn...]
    dot_general x1 -> x0, matrix products: 13 us -> none  [local(): jnp.dot(gathered, head_weight, preferred_element_type=jnp.float32)]
  transfers between devices with their start and end apart: 3 -> 0, of which waited for: 3 -> 0; matrix products, arithmetic and copies ran while one was open for 0% -> 0% of each run, Pallas kernels for 0% -> 0%
where the time goes in v1:
time: 129 us
  Pallas kernels  123 us (95%)
  local copies, waits for them, and re-layouts  5.06 us (4%)
    pallas_call x1, Pallas kernels, local(): pl.pallas_call(kernel, out_shape=(jax.ShapeDtypeStruct((2 * ROWS, WIDTH),...  123 us
    unnamed x8, local copies, waits for them, and re-layouts  5.06 us

profile of v1, /device:TPU:1, one launch (start us, length us, event | category | flops | bytes accessed | tf_op | source)
XLA Modules:
  0.0 128.9 jit_solution(14438953694127706663)
XLA Ops:
  0.6 0.0 copy-start
  0.6 1.6 %copy-done = f32[8,65536]{1,0:T(8,128)S(1)} copy-done((f32[8,65536]{1,0:T(8,128)S(1)}, f32[8,65536]{1,0:T(8,128)}, u32[]{:S(2)}) %copy-start) | copy-done | bytes 2097176
  2.2 0.0 copy-start.1
  2.2 0.9 copy-done.1
  3.1 0.0 copy-start.2
  3.1 0.7 copy-done.2
  3.8 123.1 %shard_map.59 = (f32[512,1024]{1,0:T(8,128)S(1)}, f32[2,256]{1,0:T(2,128)S(1)}) custom-call(bf16[32,1792]{1,0:T(8,128)(2,1)S(1)} %copy-done.1, bf16[1792,1024]{1,0:T(8,128)(2,1)} %w_hbm.1, f32[8,65536]{1,0:T(8,128)S(1)} %copy-done, s32[4,128]{1,0:T(4,128)S(1)} %bitcast.4), custom_call_target="tpu_custom_call" | custom-call | flops 7516192768 | bytes 16000000 | tf_op jit(solution)/shard_map/pallas_call | solution.py:484
  127.0 0.6 copy.6
  127.5 1.3 %copy.8 = f32[512,1024]{1,0:T(8,128)} copy(f32[512,1024]{1,0:T(8,128)S(1)} %get-tuple-element.8) | data formatting | bytes 4194304
Async XLA Ops:
  0.6 1.6 %copy-start = (f32[8,65536]{1,0:T(8,128)S(1)}, f32[8,65536]{1,0:T(8,128)}, u32[]{:S(2)}) copy-start(f32[8,65536]{1,0:T(8,128)} %draft_hbm.1) | copy-start | bytes 6291460
  2.2 0.9 copy-start.1
  3.1 0.7 copy-start.2

commit v2 on v1

--- a/solution.py
+++ b/solution.py
@@ -1,3 +1,5 @@
+import math
+
 import jax
 import jax.numpy as jnp
 from jax import lax
@@ -27,6 +29,8 @@
 LEVELS = 8388600.0
 STEPS = 64.0
 PACKED = 384
+LOG_STEPS = 2.0**17 / math.log(2.0)
+LOG_ZERO = 2.0**24 - 1.0
 
 ZZ, ZX, XX, XZ, SIB, AG_SEMS = 0, 8, 40, 44, 60, 68
 
@@ -50,6 +54,12 @@
     return total
 
 
+def pack4(level):
+    a, b, c, d = (level[:, 128 * k : 128 * (k + 1)] for k in range(4))
+    words = ((a << 8) | (d & 255), (b << 8) | ((d >> 8) & 255), (c << 8) | ((d >> 16) & 255))
+    return jnp.concatenate(words, axis=1)
+
+
 def unpack(words, scale):
     a, b, c = (words[:, 128 * i : 128 * (i + 1)] for i in range(3))
     d = (a & 255) | ((b & 255) << 8) | ((c << 24) >> 8)
@@ -58,7 +68,7 @@
 
 def kernel(
     hid, w_hbm, draft_hbm, ids_ref, out_hbm, acc_ref,
-    G, W, part, leg, fin, pk, dr, E, idc, colm, cola, colb, colc, colk, S,
+    G, W, part, leg, fin, pk, dbuf, dpk, dr, dd, E, idc, colm, cola, colb, colc, colk, S,
     ag_send, ag_recv, y_send, y_recv, st_send, st_recv, dr_send, dr_recv, loc,
 ):
     r = lax.axis_index("rows")
@@ -77,7 +87,8 @@
     xp, xm, xo = (x + 1) % NX, (x + NX - 1) % NX, (x + 2) % NX
     rp, rm = (r + 1) % NY, (r + NY - 1) % NY
     to_zp, to_zm = (r, vid(zp, x, c)), (r, vid(zm, x, c))
-    to_xp, to_xm = (r, vid(z, xp, c)), (r, vid(z, xm, c))
+    to_zp2, to_zm2 = (r, vid(around(2), x, c)), (r, vid(around(-2), x, c))
+    to_xp, to_xm, to_xo = (r, vid(z, xp, c)), (r, vid(z, xm, c)), (r, vid(z, xo, c))
     to_sib = (r, vid(z, x, 1 - c))
     order = [around(d) for d in (0, -1, 1, -2, 2, -3, 3, 4)]
 
@@ -85,6 +96,8 @@
     own_copy.start()
     w_copy = pltpu.make_async_copy(w_hbm, W, loc.at[1])
     w_copy.start()
+    draft_copy = pltpu.make_async_copy(draft_hbm, dbuf, loc.at[4])
+    draft_copy.start()
 
     barrier = pltpu.get_barrier_semaphore()
     for ry in (rp, rm):
@@ -119,25 +132,17 @@
 
     def zf_x_send(j):
         src = hid.at[:, ZF] if j == 0 else None
-        spread(zf(order[j], x), ZX + 4 * j, to_xp, src)
-        spread(zf(order[j], x), ZX + 4 * j + 1, to_xm, src)
-
-    def zf_x_mid(j):
-        zz = order[j]
-        arrived(zf(zz, xm), ZX + 4 * j)
-        spread(zf(zz, xm, ZF_LO), ZX + 4 * j + 2, to_xp)
-        arrived(zf(zz, xp), ZX + 4 * j + 1)
-        spread(zf(zz, xp, ZF_HI), ZX + 4 * j + 3, to_xm)
+        for k, dev in enumerate((to_xp, to_xm, to_xo)):
+            spread(zf(order[j], x), ZX + 4 * j + k, dev, src)
 
     def zf_x_end(j):
-        zz = order[j]
-        arrived(zf(zz, xo, ZF_LO), ZX + 4 * j + 2)
-        arrived(zf(zz, xo, ZF_HI), ZX + 4 * j + 3)
+        for k, xx in enumerate((xm, xp, xo)):
+            arrived(zf(order[j], xx), ZX + 4 * j + k)
 
     def zf_z(d):
         if d == 0:
-            spread(zf(z, x), ZZ, to_zp, hid.at[:, ZF])
-            spread(zf(z, x), ZZ + 1, to_zm, hid.at[:, ZF])
+            for k, dev in enumerate((to_zp, to_zm, to_zp2, to_zm2)):
+                spread(zf(z, x), ZZ + k, dev, hid.at[:, ZF])
             zf_x_send(0)
             return
         if d == 4:
@@ -147,10 +152,14 @@
             return
         za, zb = order[2 * d - 1], order[2 * d]
         arrived(zf(za, x), ZZ + 2 * d - 2)
-        spread(zf(za, x, ZF_LO if d == 3 else ZF), ZZ + 2 * d, to_zp)
+        if d == 2:
+            spread(zf(za, x), ZZ + 4, to_zp)
+            spread(zf(za, x, ZF_LO), ZZ + 6, to_zp2)
         zf_x_send(2 * d - 1)
         arrived(zf(zb, x), ZZ + 2 * d - 1)
-        spread(zf(zb, x, ZF_HI if d == 3 else ZF), ZZ + 2 * d + 1, to_zm)
+        if d == 2:
+            spread(zf(zb, x), ZZ + 5, to_zm)
+            spread(zf(zb, x, ZF_HI), ZZ + 7, to_zm2)
         zf_x_send(2 * d)
 
     def xf(xx, cols=XF):
@@ -162,7 +171,7 @@
     def xf_x_start():
         spread(xf(x), XX, to_xp, hid.at[:, XF])
         spread(xf(x), XX + 1, to_xm, hid.at[:, XF])
-        spread(xf(x), XX + 2, (r, vid(z, xo, c)), hid.at[:, XF])
+        spread(xf(x), XX + 2, to_xo, hid.at[:, XF])
 
     def xf_x_end():
         arrived(xf(xm), XX)
@@ -221,10 +230,7 @@
             unit = jnp.floor(jnp.max(jnp.abs(block), axis=1, keepdims=True) * STEPS) + 1.0
             colk[0, rows] = jnp.broadcast_to(unit, (64, 128))
             level = jnp.round(block * (LEVELS * STEPS / unit)).astype(jnp.int32)
-            a, b, c, d = (level[:, 128 * k : 128 * (k + 1)] for k in range(4))
-            dst[rows, 0:128] = (a << 8) | (d & 255)
-            dst[rows, 128:256] = (b << 8) | ((d >> 8) & 255)
-            dst[rows, 256:384] = (c << 8) | ((d >> 16) & 255)
+            dst[rows] = pack4(level)
 
         dst[ROWS : ROWS + 1, 0:ROWS] = to_lanes(colk[0])[0:1].astype(jnp.int32)
 
@@ -234,12 +240,9 @@
     def product(j):
         zz = order[j]
 
-        @pl.loop(0, 4)
-        def _(n):
-            lhs = G[zz].reshape(ROWS, FEATURES)
-            rhs = W[:, pl.ds(pl.multiple_of(n * 256, 256), 256)]
-            res = jnp.dot(lhs, rhs, preferred_element_type=F32)
-            part[zz, n // 2, :, pl.ds(pl.multiple_of((n % 2) * 256, 256), 256)] = res
+        lhs = G[zz].reshape(ROWS, FEATURES)
+        for n in range(2):
+            part[zz, n] = jnp.dot(lhs, W[:, HALF * n : HALF * (n + 1)], preferred_element_type=F32)
 
         d, q = role(zz)
 
@@ -279,18 +282,24 @@
             rows = pl.ds(pl.multiple_of(i * 64, 64), 64)
             part[zz, side, rows] = part[zz, side, rows] + unpack(leg[side, q, rows], colk[1, rows])
 
-    def onward(q):
-        for side, owner in ((0, rp), (1, rm)):
-            zz = 2 * owner + q
-            wait_recv(leg.at[side, q], y_recv.at[2 * side + q])
-            add_leg(zz, side, q)
-            pack(zz, side, pk.at[2, q, side])
-            cp = remote(
-                pk.at[2, q, side], fin.at[q, side, side], y_send.at[16 + 2 * side + q],
-                y_recv.at[8 + 2 * side + q], (owner, v),
-            )
-            cp.start()
-            sent.append(cp)
+    def steps_to(zz):
+        up, down = (zz - z + NZ) % NZ, (z - zz + NZ) % NZ
+        return jnp.minimum(up, down)
+
+    def onward(side, nth):
+        owner = (rp, rm)[side]
+        second = (steps_to(2 * owner + 1) < steps_to(2 * owner)).astype(jnp.int32)
+        q = second if nth == 0 else 1 - second
+        zz = 2 * owner + q
+        wait_recv(leg.at[side, q], y_recv.at[2 * side + q])
+        add_leg(zz, side, q)
+        pack(zz, side, pk.at[2, q, side])
+        cp = remote(
+            pk.at[2, q, side], fin.at[q, side, side], y_send.at[16 + 2 * side + q],
+            y_recv.at[8 + 2 * side + q], (owner, v),
+        )
+        cp.start()
+        sent.append(cp)
 
     def fin_wait(q):
         wait_recv(fin.at[q, 0, 1], y_recv.at[4 + q])
@@ -363,7 +372,7 @@
             rows = pl.ds(pl.multiple_of(i * 32, 32), 32)
             all_rows = pl.ds(pl.multiple_of(q * ROWS + i * 32, 32), 32)
             target = E[q, rows] * tile8(colm[q, rows])
-            draft = dr[all_rows]
+            draft = dd[all_rows]
             chosen = columns == tile8(idc[all_rows])
             excess = jnp.maximum(target - draft, 0.0)
             E[q, rows] = excess
@@ -397,30 +406,58 @@
 
     spot = dr.at[pl.ds(pl.multiple_of(v * 8, 8), 8)]
 
+    def draft_block(d):
+        return dpk.at[:, pl.ds(pl.multiple_of(d * 768, 128), 768)]
+
+    def draft_encode():
+        draft_copy.wait()
+
+        @pl.loop(0, 16)
+        def _(i):
+            block = dbuf[:, pl.ds(pl.multiple_of(i * 4096, 4096), 4096)]
+            code = jnp.round(jnp.log(block) * -LOG_STEPS)
+            code = jnp.minimum(jnp.maximum(code, 0.0), LOG_ZERO).astype(jnp.int32)
+            words = [pack4(code[:, HALF * k : HALF * (k + 1)]) for k in range(8)]
+            dpk[:, pl.ds(pl.multiple_of(i * 3072, 1024), 3072)] = jnp.concatenate(words, axis=1)
+
     def draft_send():
-        pltpu.make_async_copy(
-            draft_hbm.at[:, pl.ds(pl.multiple_of(v * WIDTH, WIDTH), WIDTH)], spot, dr_recv
-        ).start()
+        pltpu.make_async_copy(draft_block(v), spot, dr_recv).start()
 
         @pl.loop(1, NV)
         def _(k):
             d = (v + k) % NV
-            remote(
-                draft_hbm.at[:, pl.ds(pl.multiple_of(d * WIDTH, WIDTH), WIDTH)], spot, dr_send, dr_recv, (r, d)
-            ).start()
-
+            remote(draft_block(d), spot, dr_send, dr_recv, (r, d)).start()
+
+    def draft_decode():
+        pltpu.make_async_copy(dr, dr, dr_recv).wait()
+
+        @pl.loop(0, 16)
+        def _(i):
+            rows = pl.ds(pl.multiple_of(i * 32, 32), 32)
+            words = dr[rows]
+            for k in range(2):
+                w = words[:, PACKED * k : PACKED * (k + 1)]
+                a, b, c = (w[:, 128 * j : 128 * (j + 1)] for j in range(3))
+                d = (a & 255) | ((b & 255) << 8) | ((c & 255) << 16)
+                for j, code in enumerate(((a >> 8) & 0xFFFFFF, (b >> 8) & 0xFFFFFF, (c >> 8) & 0xFFFFFF, d)):
+                    code = code.astype(F32)
+                    value = jnp.where(code < LOG_ZERO, jnp.exp(code * (-1.0 / LOG_STEPS)), 0.0)
+                    dd[rows, HALF * k + 128 * j : HALF * k + 128 * (j + 1)] = value
+
+    xf_x_start()
     zf_z(0)
-    xf_x_start()
-    zf_x_mid(0)
+    draft_encode()
     own_copy.wait()
     xf_x_end()
     xf_z(0)
     zf_z(1)
+    zf_z(2)
     zf_x_end(0)
     sib(0)
-    zf_x_mid(1)
-    zf_x_mid(2)
-    zf_z(2)
+    for j in range(4):
+        idc[128 * j : 128 * j + 128] = to_rows(ids_ref[j : j + 1].astype(F32))
+    zf_z(3)
+    zf_z(4)
     w_copy.wait()
     sib_wait(0)
     product(0)
@@ -428,18 +465,10 @@
         a, b = 2 * d - 1, 2 * d
         xf_z(d)
         zf_x_end(a)
+        sib(a)
         zf_x_end(b)
-        sib(a)
         sib(b)
-        if d == 1:
-            for j in range(4):
-                idc[128 * j : 128 * j + 128] = to_rows(ids_ref[j : j + 1].astype(F32))
-        if d < 3:
-            zf_x_mid(a + 2)
-            zf_x_mid(b + 2)
-            zf_z(d + 2)
-        else:
-            zf_x_mid(7)
+        if d == 3:
             draft_send()
         sib_wait(a)
         product(a)
@@ -450,20 +479,21 @@
     sib(7)
     sib_wait(7)
     product(7)
-    onward(0)
-    onward(1)
+    for nth in range(2):
+        for side in range(2):
+            onward(side, nth)
+    draft_decode()
     fin_wait(0)
     local_stats(0)
     exchange(0, 0)
-    pltpu.make_async_copy(dr, dr, dr_recv).wait()
-    local_excess(0)
-    exchange(0, 1)
-    out0 = finish(0)
     fin_wait(1)
     local_stats(1)
     exchange(1, 0)
+    local_excess(0)
+    exchange(0, 1)
     local_excess(1)
     exchange(1, 1)
+    out0 = finish(0)
     out1 = finish(1)
 
     for cp in sent:
@@ -473,7 +503,7 @@
     for q in range(2):
         for e in range(2):
             exchange_sent(q, e)
-    some = draft_hbm.at[:, pl.ds(0, (NV - 1) * WIDTH)]
+    some = dpk.at[:, pl.ds(0, (NV - 1) * 768)]
     remote(some, some, dr_send, dr_recv, to_sib).wait_send()
     out0.wait()
     out1.wait()
@@ -496,6 +526,9 @@
             pltpu.VMEM((2, 2, ROWS + 8, PACKED), jnp.int32),
             pltpu.VMEM((2, 2, 2, ROWS + 8, PACKED), jnp.int32),
             pltpu.VMEM((3, 2, 2, ROWS + 8, PACKED), jnp.int32),
+            pltpu.VMEM((8, NV * WIDTH), F32),
+            pltpu.VMEM((8, NV * 768), jnp.int32),
+            pltpu.VMEM((2 * ROWS, 768), jnp.int32),
             pltpu.VMEM((2 * ROWS, WIDTH), F32),
             pltpu.VMEM((2, ROWS, WIDTH), F32),
             pltpu.VMEM((2 * ROWS, 128), F32),
@@ -513,7 +546,7 @@
             dma((2, 2)),
             dma,
             dma,
-            dma((4,)),
+            dma((5,)),
         ],
         compiler_params=pltpu.CompilerParams(
             collective_id=0, has_side_effects=True, vmem_limit_bytes=48 * 1024 * 1024

time: 129 us -> 117 us (0.907)
  Pallas kernels: 123 us -> 111 us
    pallas_call x1, Pallas kernels: 123 us -> 111 us  [local(): pl.pallas_call(kernel, out_shape=(jax.ShapeDtypeStruct((2 * ROWS, WIDTH),...]
where the time goes in v2:
time: 117 us; the launch traced here: 116 us
  Pallas kernels  111 us (95%)
  local copies, waits for them, and re-layouts  5.06 us (4%)
    pallas_call x1, Pallas kernels, local(): pl.pallas_call(kernel, out_shape=(jax.ShapeDtypeStruct((2 * ROWS, WIDTH),...  111 us
    unnamed x8, local copies, waits for them, and re-layouts  5.06 us

profile of v2, /device:TPU:1, one launch (start us, length us, event | category | flops | bytes accessed | tf_op | source)
XLA Modules:
  0.0 116.4 jit_solution(724288628629877785)
XLA Ops:
  0.6 0.0 copy-start
  0.6 1.6 %copy-done = f32[8,65536]{1,0:T(8,128)S(1)} copy-done((f32[8,65536]{1,0:T(8,128)S(1)}, f32[8,65536]{1,0:T(8,128)}, u32[]{:S(2)}) %copy-start) | copy-done | bytes 2097176
  2.2 0.0 copy-start.1
  2.2 0.9 copy-done.1
  3.1 0.0 copy-start.2
  3.1 0.7 copy-done.2
  3.8 110.7 %shard_map.59 = (f32[512,1024]{1,0:T(8,128)S(1)}, f32[2,256]{1,0:T(2,128)S(1)}) custom-call(bf16[32,1792]{1,0:T(8,128)(2,1)S(1)} %copy-done.1, bf16[1792,1024]{1,0:T(8,128)(2,1)} %w_hbm.1, f32[8,65536]{1,0:T(8,128)S(1)} %copy-done, s32[4,128]{1,0:T(4,128)S(1)} %bitcast.4), custom_call_target="tpu_custom_call" | custom-call | flops 7516192768 | bytes 16000000 | tf_op jit(solution)/shard_map/pallas_call | solution.py:514
  114.5 0.6 copy.6
  115.1 1.3 %copy.8 = f32[512,1024]{1,0:T(8,128)} copy(f32[512,1024]{1,0:T(8,128)S(1)} %get-tuple-element.8) | data formatting | bytes 4194304
Async XLA Ops:
  0.6 1.6 %copy-start = (f32[8,65536]{1,0:T(8,128)S(1)}, f32[8,65536]{1,0:T(8,128)}, u32[]{:S(2)}) copy-start(f32[8,65536]{1,0:T(8,128)} %draft_hbm.1) | copy-start | bytes 6291460
  2.2 0.9 copy-start.1
  3.1 0.7 copy-start.2

commit v3 on v2

--- a/solution.py
+++ b/solution.py
@@ -100,14 +100,10 @@
     draft_copy.start()
 
     barrier = pltpu.get_barrier_semaphore()
-    for ry in (rp, rm):
-        pl.semaphore_signal(barrier, inc=1, device_id=(ry, v), device_id_type=MESH)
-
-    @pl.loop(1, NV)
-    def _(k):
-        pl.semaphore_signal(barrier, inc=1, device_id=(r, (v + k) % NV), device_id_type=MESH)
-
-    pl.semaphore_wait(barrier, NV + 1)
+    near = (to_zp, to_zm, to_zp2, to_zm2, to_xp, to_xm, to_xo, to_sib, (rp, v), (rm, v))
+    for dev in near:
+        pl.semaphore_signal(barrier, inc=1, device_id=dev, device_id_type=MESH)
+    pl.semaphore_wait(barrier, len(near))
 
     sent = []
 
@@ -210,6 +206,15 @@
     def role(zz):
         return (zz // 2 - r + NY) % NY, zz % 2
 
+    odd = z % 2
+    far_down = (role(around(-2))[0] == 2).astype(jnp.int32)
+    far_up = (role(around(2))[0] == 2).astype(jnp.int32)
+    work = [z]
+    for d in (1, 2, 3):
+        up = odd if d != 2 else odd * far_up + (1 - odd) * (1 - far_down)
+        work += [around(d * (2 * up - 1)), around(-d * (2 * up - 1))]
+    work.append(order[7])
+
     def far_left(q, j):
         return remote(pk.at[0, q, 0], leg.at[0, q], y_send.at[2 * j], y_recv.at[q], (rp, v))
 
@@ -238,7 +243,7 @@
         colk[k] = to_rows(src[ROWS : ROWS + 1, 0:ROWS].astype(F32)) * (1.0 / (LEVELS * STEPS))
 
     def product(j):
-        zz = order[j]
+        zz = work[j]
 
         lhs = G[zz].reshape(ROWS, FEATURES)
         for n in range(2):
@@ -264,7 +269,7 @@
             near_left(q, j).start()
 
     def product_sent(j):
-        d, q = role(order[j])
+        d, q = role(work[j])
 
         @pl.when(d >= 2)
         def _():
@@ -468,17 +473,16 @@
         sib(a)
         zf_x_end(b)
         sib(b)
-        if d == 3:
-            draft_send()
         sib_wait(a)
+        sib_wait(b)
         product(a)
-        sib_wait(b)
         product(b)
     xf_z(4)
     zf_x_end(7)
     sib(7)
     sib_wait(7)
     product(7)
+    draft_send()
     for nth in range(2):
         for side in range(2):
             onward(side, nth)
@@ -549,7 +553,7 @@
             dma((5,)),
         ],
         compiler_params=pltpu.CompilerParams(
-            collective_id=0, has_side_effects=True, vmem_limit_bytes=48 * 1024 * 1024
+            collective_id=0, has_side_effects=True, vmem_limit_bytes=50 * 1024 * 1024
         ),
         cost_estimate=pl.CostEstimate(flops=7_516_192_768, bytes_accessed=16_000_000, transcendentals=524_288),
     )(hidden, head_weight, draft_probs, draft_ids.reshape(4, 128))

time: 117 us -> 111 us (0.949)
  Pallas kernels: 111 us -> 107 us
  local copies, waits for them, and re-layouts: 5.06 us -> 3.47 us
    pallas_call x1, Pallas kernels: 111 us -> 107 us  [local(): pl.pallas_call(kernel, out_shape=(jax.ShapeDtypeStruct((2 * ROWS, WIDTH),...]
    unnamed x8 -> x6, local copies, waits for them, and re-layouts: 5.06 us -> 3.47 us
where the time goes in v3:
time: 111 us
  Pallas kernels  107 us (96%)
  local copies, waits for them, and re-layouts  3.47 us (3%)
    pallas_call x1, Pallas kernels, local(): pl.pallas_call(kernel, out_shape=(jax.ShapeDtypeStruct((2 * ROWS, WIDTH),...  107 us
    unnamed x6, local copies, waits for them, and re-layouts  3.47 us

profile of v3, /device:TPU:1, one launch (start us, length us, event | category | flops | bytes accessed | tf_op | source)
XLA Modules:
  0.0 111.1 jit_solution(11499501716722627590)
XLA Ops:
  0.6 0.0 copy-start
  0.6 0.9 copy-done
  1.5 0.0 copy-start.1
  1.5 0.7 copy-done.1
  2.2 106.9 %shard_map.59 = (f32[512,1024]{1,0:T(8,128)S(1)}, f32[2,256]{1,0:T(2,128)S(1)}) custom-call(bf16[32,1792]{1,0:T(8,128)(2,1)S(1)} %copy-done, bf16[1792,1024]{1,0:T(8,128)(2,1)} %w_hbm.1, f32[8,65536]{1,0:T(8,128)} %draft_hbm.1, s32[4,128]{1,0:T(4,128)S(1)} %bitcast.4), custom_call_target="tpu_custom_call" | custom-call | flops 7516192768 | bytes 16000000 | tf_op jit(solution)/shard_map/pallas_call | solution.py:518
  109.2 0.6 copy.6
  109.7 1.3 %copy.8 = f32[512,1024]{1,0:T(8,128)} copy(f32[512,1024]{1,0:T(8,128)S(1)} %get-tuple-element.8) | data formatting | bytes 4194304
Async XLA Ops:
  0.6 0.9 copy-start
  1.5 0.7 copy-start.1

commit v4 on v3

--- a/solution.py
+++ b/solution.py
@@ -67,7 +67,7 @@
 
 
 def kernel(
-    hid, w_hbm, draft_hbm, ids_ref, out_hbm, acc_ref,
+    hid, w_hbm, draft_hbm, ids_ref, out_hbm, acc_ref, inv_ref,
     G, W, part, leg, fin, pk, dbuf, dpk, dr, dd, E, idc, colm, cola, colb, colc, colk, S,
     ag_send, ag_recv, y_send, y_recv, st_send, st_recv, dr_send, dr_recv, loc,
 ):
@@ -315,7 +315,7 @@
     def exchange(q, e):
         mine = S.at[q, e, v]
 
-        @pl.loop(0, NZ)
+        @pl.loop(0, NZ, unroll=True)
         def _(i):
             dz = 4 + (1 - 2 * (i % 2)) * ((i + 1) // 2)
             zz = (z + dz) % NZ
@@ -398,13 +398,9 @@
         exchange_wait(q, 1)
         both = jnp.sum(S[q, 1], axis=0)
         acc_ref[q : q + 1] = both[:, ROWS : 2 * ROWS]
-        colm[q] = to_rows(1.0 / jnp.maximum(both[:, 0:ROWS], mass_floor))
-
-        @pl.loop(0, 8)
-        def _(i):
-            rows = pl.ds(pl.multiple_of(i * 32, 32), 32)
-            E[q, rows] = E[q, rows] * tile8(colm[q, rows])
-
+        inv_ref[q : q + 1] = 1.0 / jnp.maximum(both[:, 0:ROWS], mass_floor)
+
+    def leave(q):
         cp = pltpu.make_async_copy(E.at[q], out_hbm.at[pl.ds(q * ROWS, ROWS)], loc.at[2 + q])
         cp.start()
         return cp
@@ -428,7 +424,7 @@
     def draft_send():
         pltpu.make_async_copy(draft_block(v), spot, dr_recv).start()
 
-        @pl.loop(1, NV)
+        @pl.loop(1, NV, unroll=7)
         def _(k):
             d = (v + k) % NV
             remote(draft_block(d), spot, dr_send, dr_recv, (r, d)).start()
@@ -486,19 +482,21 @@
     for nth in range(2):
         for side in range(2):
             onward(side, nth)
-    draft_decode()
     fin_wait(0)
     local_stats(0)
     exchange(0, 0)
     fin_wait(1)
     local_stats(1)
     exchange(1, 0)
+    draft_decode()
     local_excess(0)
     exchange(0, 1)
     local_excess(1)
     exchange(1, 1)
-    out0 = finish(0)
-    out1 = finish(1)
+    out0 = leave(0)
+    out1 = leave(1)
+    finish(0)
+    finish(1)
 
     for cp in sent:
         cp.wait_send()
@@ -515,14 +513,15 @@
 
 def local(hidden, head_weight, draft_probs, draft_ids):
     dma = pltpu.SemaphoreType.DMA
-    residual, accept = pl.pallas_call(
+    excess, accept, inverse = pl.pallas_call(
         kernel,
         out_shape=(
             jax.ShapeDtypeStruct((2 * ROWS, WIDTH), F32),
             jax.ShapeDtypeStruct((2, ROWS), F32),
+            jax.ShapeDtypeStruct((2, ROWS), F32),
         ),
         in_specs=[pl.BlockSpec(memory_space=pltpu.HBM)] * 3 + [pl.BlockSpec(memory_space=pltpu.VMEM)],
-        out_specs=(pl.BlockSpec(memory_space=pltpu.HBM), pl.BlockSpec(memory_space=pltpu.VMEM)),
+        out_specs=(pl.BlockSpec(memory_space=pltpu.HBM),) + (pl.BlockSpec(memory_space=pltpu.VMEM),) * 2,
         scratch_shapes=[
             pltpu.VMEM((NZ, NX, NC, SHARD, FEATURES), jnp.bfloat16),
             pltpu.VMEM((FEATURES, WIDTH), jnp.bfloat16),
@@ -557,7 +556,7 @@
         ),
         cost_estimate=pl.CostEstimate(flops=7_516_192_768, bytes_accessed=16_000_000, transcendentals=524_288),
     )(hidden, head_weight, draft_probs, draft_ids.reshape(4, 128))
-    return residual, accept.reshape(2 * ROWS)
+    return excess * inverse.reshape(2 * ROWS, 1), accept.reshape(2 * ROWS)
 
 
 def solution(mesh):

time: 111 us -> 111 us (level)
  other arithmetic: 0 us -> 1.52 us
  local copies, waits for them, and re-layouts: 3.47 us -> 2.15 us
    mul x0 -> x1, other arithmetic: none -> 1.52 us  [local(): return (excess * inverse.reshape(2 * ROWS, 1), accept.reshape(2 * ROWS))]
    unnamed x6, local copies, waits for them, and re-layouts: 3.47 us -> 2.15 us
where the time goes in v4:
time: 111 us; the launch traced here: 110 us
  Pallas kernels  106 us (95%)
  local copies, waits for them, and re-layouts  2.15 us (2%)
  other arithmetic  1.52 us (1%)
    pallas_call x1, Pallas kernels, local(): pl.pallas_call(kernel, out_shape=(jax.ShapeDtypeStruct((2 * ROWS, WIDTH),...  106 us

profile of v4, /device:TPU:1, one launch (start us, length us, event | category | flops | bytes accessed | tf_op | source)
XLA Modules:
  0.0 110.5 jit_solution(17552971523293825018)
XLA Ops:
  0.6 0.0 copy-start
  0.6 0.9 copy-done
  1.5 0.0 copy-start.1
  1.5 0.7 copy-done.1
  2.2 106.2 %shard_map.59 = (f32[512,1024]{1,0:T(8,128)S(1)}, f32[2,256]{1,0:T(2,128)S(1)}, f32[2,256]{1,0:T(2,128)S(1)}) custom-call(bf16[32,1792]{1,0:T(8,128)(2,1)S(1)} %copy-done, bf16[1792,1024]{1,0:T(8,128)(2,1)} %w_hbm.1, f32[8,65536]{1,0:T(8,128)} %draft_hbm.1, s32[4,128]{1,0:T(4,128)S(1)} %bitcast.7), custom_call_target="tpu_custom_call" | custom-call | flops 7516192768 | bytes 16000000 | tf_op jit(solution)/shard_map/pallas_call | solution.py:516
  108.4 1.5 %broadcast_multiply_fusion = f32[512,1024]{1,0:T(8,128)} fusion(f32[512,1024]{1,0:T(8,128)S(1)} %get-tuple-element.5, f32[512]{0:T(512)S(1)} %bitcast.8), kind=kLoop, calls=%fused_computation | loop fusion | flops 524288 | bytes 4196352 | tf_op jit(solution)/shard_map/mul | solution.py:559
  109.9 0.6 copy.7
  (1 shorter events, 0.0 us)
Async XLA Ops:
  0.6 0.9 copy-start
  1.5 0.7 copy-start.1
